TPU v7x, 32 devices: a whole 2x2x4 slice. The times are simulated.
32 devices in a mesh: dp: 4 (over y, x), fsdp: 8 (over z, core).
Axes of the slice: x: 2, y: 2, z: 4, core: 2. Of those that a mesh axis runs over, the one named last changes fastest.
Arguments:
- latents: bfloat16 [32, 128, 1024], P(('dp', 'fsdp')), may hold values from -6 to 6
- inputs: bfloat16 [32, 1024, 1024], P(('dp', 'fsdp')), may hold values from -6 to 6
- frames: int32 [32], P(('dp', 'fsdp')), may hold values from 4 to 16, as said below
- norm_latent: float32 [1024], P(('dp', 'fsdp')), may hold values from 0.5 to 1.5
- norm_input: float32 [1024], P(('dp', 'fsdp')), may hold values from 0.5 to 1.5
- cross_query: float32 [1024, 1024], P(('dp', 'fsdp')), may hold values from -0.1875 to 0.1875
- cross_key: float32 [1024, 1024], P(('dp', 'fsdp')), may hold values from -0.1875 to 0.1875
- cross_value: float32 [1024, 1024], P(('dp', 'fsdp')), may hold values from -0.1875 to 0.1875
- cross_output: float32 [1024, 1024], P(('dp', 'fsdp')), may hold values from -2 to 2
- norm_first: float32 [1024], P(('dp', 'fsdp')), may hold values from 0.5 to 1.5
- first_up: float32 [1024, 4096], P(('dp', 'fsdp')), may hold values from -0.1875 to 0.1875
- first_down: float32 [4096, 1024], P(('dp', 'fsdp')), may hold values from -0.09375 to 0.09375
- norm_self: float32 [1024], P(('dp', 'fsdp')), may hold values from 0.5 to 1.5
- self_query: float32 [1024, 1024], P(('dp', 'fsdp')), may hold values from -0.1875 to 0.1875
- self_key: float32 [1024, 1024], P(('dp', 'fsdp')), may hold values from -0.1875 to 0.1875
- self_value: float32 [1024, 1024], P(('dp', 'fsdp')), may hold values from -0.1875 to 0.1875
- self_output: float32 [1024, 1024], P(('dp', 'fsdp')), may hold values from -1 to 1
- norm_second: float32 [1024], P(('dp', 'fsdp')), may hold values from 0.5 to 1.5
- second_up: float32 [1024, 4096], P(('dp', 'fsdp')), may hold values from -0.1875 to 0.1875
- second_down: float32 [4096, 1024], P(('dp', 'fsdp')), may hold values from -0.09375 to 0.09375
- cotangent: bfloat16 [32, 128, 1024], P(('dp', 'fsdp')), may hold values from -6 to 6
Outputs:
- out_latents: bfloat16 [32, 128, 1024], P(('dp', 'fsdp'))
- grad_latents: bfloat16 [32, 128, 1024], P(('dp', 'fsdp'))
- grad_inputs: bfloat16 [32, 1024, 1024], P(('dp', 'fsdp'))
- grad_norm_latent: float32 [1024], P(('dp', 'fsdp'))
- grad_norm_input: float32 [1024], P(('dp', 'fsdp'))
- grad_cross_query: float32 [1024, 1024], P(('dp', 'fsdp'))
- grad_cross_key: float32 [1024, 1024], P(('dp', 'fsdp'))
- grad_cross_value: float32 [1024, 1024], P(('dp', 'fsdp'))
- grad_cross_output: float32 [1024, 1024], P(('dp', 'fsdp'))
- grad_norm_first: float32 [1024], P(('dp', 'fsdp'))
- grad_first_up: float32 [1024, 4096], P(('dp', 'fsdp'))
- grad_first_down: float32 [4096, 1024], P(('dp', 'fsdp'))
- grad_norm_self: float32 [1024], P(('dp', 'fsdp'))
- grad_self_query: float32 [1024, 1024], P(('dp', 'fsdp'))
- grad_self_key: float32 [1024, 1024], P(('dp', 'fsdp'))
- grad_self_value: float32 [1024, 1024], P(('dp', 'fsdp'))
- grad_self_output: float32 [1024, 1024], P(('dp', 'fsdp'))
- grad_norm_second: float32 [1024], P(('dp', 'fsdp'))
- grad_second_up: float32 [1024, 4096], P(('dp', 'fsdp'))
- grad_second_down: float32 [4096, 1024], P(('dp', 'fsdp'))
Inputs may be any that keep to these rules, and one draw needn't show every extreme that they name: Each entry of frames is 4 or 16 (nothing in between); in every draw some group has 4 frames and some has 16.
All inputs are finite; a program needn't handle non-finite values.
Results may differ from a plain program's by a relative error of at most 0.024.
Values may be sent and summed in bfloat16 or wider, within the bound.
A program may use at most 256 MiB of HBM per device.

v0:
```python
import jax
import jax.numpy as jnp
from jax import lax
from jax.sharding import PartitionSpec as P

HEADS = 8
FRAME_TOK = 64


EPS = 1e-05
NEG = -1000000000.0
FOLD = 8


def layer_norm(value, gain):
    center = value - jnp.mean(value, axis=-1, keepdims=True)
    spread = jnp.mean(center * center, axis=-1, keepdims=True)
    return center * lax.rsqrt(spread + EPS) * gain


def activate(value):
    return jax.nn.gelu(value, approximate=True)


def product(left, right):
    return jnp.dot(left, right, preferred_element_type=jnp.float32)


def weight_grad(left, right):
    return lax.dot_general(
        left, right, (((0,), (0,)), ((), ())), preferred_element_type=jnp.float32
    )


def back_product(grad, weight):
    return lax.dot_general(
        grad, weight, (((1,), (1,)), ((), ())), preferred_element_type=jnp.float32
    )


def widen(value):
    return value.reshape(value.shape[0] * FOLD, value.shape[1] // FOLD)


def narrow(value, columns):
    return value.reshape(-1, columns)


def norm_back(value, gain, grad):
    _, pull = jax.vjp(layer_norm, value, gain)
    return pull(grad)


def activate_back(value, grad):
    _, pull = jax.vjp(activate, value)
    return pull(grad)[0]


def split_heads(value, groups):
    return value.reshape(groups, -1, HEADS, value.shape[-1] // HEADS)


def merge_heads(value):
    return value.reshape(-1, value.shape[2] * value.shape[3])


def masked_scores(query, key, valid):
    scale = query.shape[-1] ** (-0.5)
    scores = jnp.einsum("gqhd,gkhd->ghqk", query, key, preferred_element_type=jnp.float32) * scale
    return jnp.where(valid[:, None, None, :], scores, NEG)


def attend_forward(query, key, value, valid):
    scores = masked_scores(query, key, valid)
    top = jnp.max(scores, axis=-1, keepdims=True)
    expo = jnp.exp(scores - top)
    denom = jnp.sum(expo, axis=-1, keepdims=True)
    weights = (expo / denom).astype(jnp.bfloat16)
    mixed = jnp.einsum("ghqk,gkhd->gqhd", weights, value, preferred_element_type=jnp.float32)
    return (merge_heads(mixed).astype(jnp.bfloat16), top + jnp.log(denom))


def attend_back(query, key, value, valid, logsum, grad_mixed):
    scale = query.shape[-1] ** (-0.5)
    probs = jnp.exp(masked_scores(query, key, valid) - logsum)
    grad_probs = jnp.einsum(
        "gqhd,gkhd->ghqk", grad_mixed, value, preferred_element_type=jnp.float32
    )
    inner = jnp.sum(probs * grad_probs, axis=-1, keepdims=True)
    grad_scores = (probs * (grad_probs - inner)).astype(jnp.bfloat16)
    weights = probs.astype(jnp.bfloat16)
    grad_query = (
        jnp.einsum("ghqk,gkhd->gqhd", grad_scores, key, preferred_element_type=jnp.float32) * scale
    )
    grad_key = (
        jnp.einsum("ghqk,gqhd->gkhd", grad_scores, query, preferred_element_type=jnp.float32)
        * scale
    )
    grad_value = jnp.einsum(
        "ghqk,gqhd->gkhd", weights, grad_mixed, preferred_element_type=jnp.float32
    )
    return (
        merge_heads(grad_query).astype(jnp.bfloat16),
        merge_heads(grad_key).astype(jnp.bfloat16),
        merge_heads(grad_value).astype(jnp.bfloat16),
    )


def feed_forward(resid, gain, w_up, w_down):
    normed = layer_norm(resid, gain.astype(jnp.float32)).astype(jnp.bfloat16)
    before = product(normed, w_up)
    hidden = activate(before).astype(jnp.bfloat16)
    return (resid + product(hidden, w_down), (normed, before, hidden))


def feed_back(grad, resid, gain, saved, w_up, w_down):
    normed, before, hidden = saved
    grad_low = grad.astype(jnp.bfloat16)
    grad_down = weight_grad(hidden, grad_low)
    grad_before = activate_back(before, back_product(grad_low, w_down)).astype(jnp.bfloat16)
    grad_up = weight_grad(normed, grad_before)
    grad_resid, grad_gain = norm_back(
        resid, gain.astype(jnp.float32), back_product(grad_before, w_up)
    )
    return (grad + grad_resid, grad_gain, grad_up, grad_down)


def project_back(grad, mixed, w_out, query, key, value, valid, logsum, groups):
    grad_low = grad.astype(jnp.bfloat16)
    grad_out = weight_grad(mixed, grad_low)
    grad_mixed = back_product(grad_low, w_out).astype(jnp.bfloat16)
    grad_query, grad_key, grad_value = attend_back(
        split_heads(query, groups),
        split_heads(key, groups),
        split_heads(value, groups),
        valid,
        logsum,
        split_heads(grad_mixed, groups),
    )
    return (grad_out, grad_query, grad_key, grad_value)


def local(
    latents,
    inputs,
    frames,
    norm_latent,
    norm_input,
    cross_query,
    cross_key,
    cross_value,
    cross_output,
    norm_first,
    first_up,
    first_down,
    norm_self,
    self_query,
    self_key,
    self_value,
    self_output,
    norm_second,
    second_up,
    second_down,
    cotangent,
):
    groups, lat_rows, width = latents.shape
    span = inputs.shape[1]
    hidden_width = first_up.shape[1]
    low_type = jnp.bfloat16
    cross_set = (
        lax.all_gather(norm_latent.astype(low_type), ("dp", "fsdp"), axis=0, tiled=True),
        lax.all_gather(norm_input.astype(low_type), ("dp", "fsdp"), axis=0, tiled=True),
        lax.all_gather(cross_query.astype(low_type), ("dp", "fsdp"), axis=0, tiled=True),
        lax.all_gather(cross_key.astype(low_type), ("dp", "fsdp"), axis=0, tiled=True),
        lax.all_gather(cross_value.astype(low_type), ("dp", "fsdp"), axis=0, tiled=True),
        lax.all_gather(cross_output.astype(low_type), ("dp", "fsdp"), axis=0, tiled=True),
        lax.all_gather(norm_first.astype(low_type), ("dp", "fsdp"), axis=0, tiled=True),
        lax.all_gather(first_up.astype(low_type), ("dp", "fsdp"), axis=0, tiled=True),
        lax.all_gather(first_down.astype(low_type), ("dp", "fsdp"), axis=0, tiled=True),
    )
    gain_lat, gain_inp, w_query, w_key, w_value, w_out, gain_first, up_one, down_one = cross_set
    positions = jnp.arange(span, dtype=jnp.int32)
    valid = positions[None, :] < (frames * FRAME_TOK)[:, None]
    every = jnp.ones((groups, lat_rows), dtype=bool)
    latent_rows = latents.reshape(groups * lat_rows, width).astype(jnp.float32)
    input_rows = inputs.reshape(groups * span, width).astype(jnp.float32)
    normed_lat = layer_norm(latent_rows, gain_lat.astype(jnp.float32)).astype(low_type)
    normed_inp = layer_norm(input_rows, gain_inp.astype(jnp.float32)).astype(low_type)
    query_one = product(normed_lat, w_query).astype(low_type)
    key_one = product(normed_inp, w_key).astype(low_type)
    value_one = product(normed_inp, w_value).astype(low_type)
    mixed_one, logsum_one = attend_forward(
        split_heads(query_one, groups),
        split_heads(key_one, groups),
        split_heads(value_one, groups),
        valid,
    )
    first_resid = latent_rows + product(mixed_one, w_out)
    second_resid, saved_one = feed_forward(first_resid, gain_first, up_one, down_one)
    self_set = (
        lax.all_gather(norm_self.astype(low_type), ("dp", "fsdp"), axis=0, tiled=True),
        lax.all_gather(self_query.astype(low_type), ("dp", "fsdp"), axis=0, tiled=True),
        lax.all_gather(self_key.astype(low_type), ("dp", "fsdp"), axis=0, tiled=True),
        lax.all_gather(self_value.astype(low_type), ("dp", "fsdp"), axis=0, tiled=True),
        lax.all_gather(self_output.astype(low_type), ("dp", "fsdp"), axis=0, tiled=True),
        lax.all_gather(norm_second.astype(low_type), ("dp", "fsdp"), axis=0, tiled=True),
        lax.all_gather(second_up.astype(low_type), ("dp", "fsdp"), axis=0, tiled=True),
        lax.all_gather(second_down.astype(low_type), ("dp", "fsdp"), axis=0, tiled=True),
    )
    gain_self, s_query, s_key, s_value, s_out, gain_second, up_two, down_two = self_set
    normed_self = layer_norm(second_resid, gain_self.astype(jnp.float32)).astype(low_type)
    query_two = product(normed_self, s_query).astype(low_type)
    key_two = product(normed_self, s_key).astype(low_type)
    value_two = product(normed_self, s_value).astype(low_type)
    mixed_two, logsum_two = attend_forward(
        split_heads(query_two, groups),
        split_heads(key_two, groups),
        split_heads(value_two, groups),
        every,
    )
    third_resid = second_resid + product(mixed_two, s_out)
    final_resid, saved_two = feed_forward(third_resid, gain_second, up_two, down_two)
    result = final_resid.reshape(groups, lat_rows, width).astype(low_type)
    grad_final = cotangent.reshape(groups * lat_rows, width).astype(jnp.float32)
    grad_third, grad_gain_second, grad_up_two, grad_down_two = feed_back(
        grad_final, third_resid, gain_second, saved_two, up_two, down_two
    )
    grad_s_out, grad_query_two, grad_key_two, grad_value_two = project_back(
        grad_third, mixed_two, s_out, query_two, key_two, value_two, every, logsum_two, groups
    )
    grad_s_query = weight_grad(normed_self, grad_query_two)
    grad_s_key = weight_grad(normed_self, grad_key_two)
    grad_s_value = weight_grad(normed_self, grad_value_two)
    grad_normed_self = (
        back_product(grad_query_two, s_query)
        + back_product(grad_key_two, s_key)
        + back_product(grad_value_two, s_value)
    )
    grad_from_self, grad_gain_self = norm_back(
        second_resid, gain_self.astype(jnp.float32), grad_normed_self
    )
    grad_second = grad_third + grad_from_self
    grad_first, grad_gain_first, grad_up_one, grad_down_one = feed_back(
        grad_second, first_resid, gain_first, saved_one, up_one, down_one
    )
    grad_w_out, grad_query_one, grad_key_one, grad_value_one = project_back(
        grad_first, mixed_one, w_out, query_one, key_one, value_one, valid, logsum_one, groups
    )
    grad_w_query = weight_grad(normed_lat, grad_query_one)
    grad_w_key = weight_grad(normed_inp, grad_key_one)
    grad_w_value = weight_grad(normed_inp, grad_value_one)
    grad_from_lat, grad_gain_lat = norm_back(
        latent_rows, gain_lat.astype(jnp.float32), back_product(grad_query_one, w_query)
    )
    grad_latent_rows = grad_first + grad_from_lat
    grad_normed_inp = back_product(grad_key_one, w_key) + back_product(grad_value_one, w_value)
    grad_input_rows, grad_gain_inp = norm_back(
        input_rows, gain_inp.astype(jnp.float32), grad_normed_inp
    )
    every_sum = (
        lax.psum_scatter(grad_gain_lat, ("dp", "fsdp"), scatter_dimension=0, tiled=True),
        lax.psum_scatter(grad_gain_inp, ("dp", "fsdp"), scatter_dimension=0, tiled=True),
        lax.psum_scatter(widen(grad_w_query), ("dp", "fsdp"), scatter_dimension=0, tiled=True),
        lax.psum_scatter(widen(grad_w_key), ("dp", "fsdp"), scatter_dimension=0, tiled=True),
        lax.psum_scatter(widen(grad_w_value), ("dp", "fsdp"), scatter_dimension=0, tiled=True),
        lax.psum_scatter(widen(grad_w_out), ("dp", "fsdp"), scatter_dimension=0, tiled=True),
        lax.psum_scatter(grad_gain_first, ("dp", "fsdp"), scatter_dimension=0, tiled=True),
        lax.psum_scatter(widen(grad_up_one), ("dp", "fsdp"), scatter_dimension=0, tiled=True),
        lax.psum_scatter(widen(grad_down_one), ("dp", "fsdp"), scatter_dimension=0, tiled=True),
        lax.psum_scatter(grad_gain_self, ("dp", "fsdp"), scatter_dimension=0, tiled=True),
        lax.psum_scatter(widen(grad_s_query), ("dp", "fsdp"), scatter_dimension=0, tiled=True),
        lax.psum_scatter(widen(grad_s_key), ("dp", "fsdp"), scatter_dimension=0, tiled=True),
        lax.psum_scatter(widen(grad_s_value), ("dp", "fsdp"), scatter_dimension=0, tiled=True),
        lax.psum_scatter(widen(grad_s_out), ("dp", "fsdp"), scatter_dimension=0, tiled=True),
        lax.psum_scatter(grad_gain_second, ("dp", "fsdp"), scatter_dimension=0, tiled=True),
        lax.psum_scatter(widen(grad_up_two), ("dp", "fsdp"), scatter_dimension=0, tiled=True),
        lax.psum_scatter(widen(grad_down_two), ("dp", "fsdp"), scatter_dimension=0, tiled=True),
    )
    grad_latents = grad_latent_rows.reshape(groups, lat_rows, width).astype(low_type)
    grad_inputs = grad_input_rows.reshape(groups, span, width).astype(low_type)
    return (
        result,
        grad_latents,
        grad_inputs,
        every_sum[0],
        every_sum[1],
        narrow(every_sum[2], width),
        narrow(every_sum[3], width),
        narrow(every_sum[4], width),
        narrow(every_sum[5], width),
        every_sum[6],
        narrow(every_sum[7], hidden_width),
        narrow(every_sum[8], width),
        every_sum[9],
        narrow(every_sum[10], width),
        narrow(every_sum[11], width),
        narrow(every_sum[12], width),
        narrow(every_sum[13], width),
        every_sum[14],
        narrow(every_sum[15], hidden_width),
        narrow(every_sum[16], width),
    )


def solution(mesh):
    in_specs = (
        P(("dp", "fsdp"), None, None),
        P(("dp", "fsdp"), None, None),
        P(("dp", "fsdp")),
        P(("dp", "fsdp")),
        P(("dp", "fsdp")),
        P(("dp", "fsdp"), None),
        P(("dp", "fsdp"), None),
        P(("dp", "fsdp"), None),
        P(("dp", "fsdp"), None),
        P(("dp", "fsdp")),
        P(("dp", "fsdp"), None),
        P(("dp", "fsdp"), None),
        P(("dp", "fsdp")),
        P(("dp", "fsdp"), None),
        P(("dp", "fsdp"), None),
        P(("dp", "fsdp"), None),
        P(("dp", "fsdp"), None),
        P(("dp", "fsdp")),
        P(("dp", "fsdp"), None),
        P(("dp", "fsdp"), None),
        P(("dp", "fsdp"), None, None),
    )
    out_specs = (
        P(("dp", "fsdp"), None, None),
        P(("dp", "fsdp"), None, None),
        P(("dp", "fsdp"), None, None),
        P(("dp", "fsdp")),
        P(("dp", "fsdp")),
        P(("dp", "fsdp"), None),
        P(("dp", "fsdp"), None),
        P(("dp", "fsdp"), None),
        P(("dp", "fsdp"), None),
        P(("dp", "fsdp")),
        P(("dp", "fsdp"), None),
        P(("dp", "fsdp"), None),
        P(("dp", "fsdp")),
        P(("dp", "fsdp"), None),
        P(("dp", "fsdp"), None),
        P(("dp", "fsdp"), None),
        P(("dp", "fsdp"), None),
        P(("dp", "fsdp")),
        P(("dp", "fsdp"), None),
        P(("dp", "fsdp"), None),
    )
    return jax.shard_map(local, mesh=mesh, in_specs=in_specs, out_specs=out_specs, check_vma=False)
```

profile of v0, /device:TPU:0, one launch (start us, length us, event | category | flops | bytes accessed | tf_op | source)
XLA Modules:
  0.0 2752.7 jit_solution(4557216884468586468)
XLA Ops:
  23.1 42.4 %all-reduce.11 = (bf16[1024]{0:T(1024)(128)(2,1)S(1)}, bf16[1024]{0:T(1024)(128)(2,1)S(1)}, bf16[1024]{0:T(1024)(128)(2,1)S(1)}, bf16[1024]{0:T(1024)(128)(2,1)S(1)}, bf16[1024]{0:T(1024)(128)(2,1)S(1)}) all-reduce(bf16[1024]{0:T(1024)(128)(2,1)S(1)} %dynamic-update-slice, ...), channel_id=1, replica_groups=mesh['dp'=4,'fsdp'=8] {'dp','fsdp'}, use_global_device_ids=true, to_apply=%add | all-reduce | flops 5120 | bytes 20480
  73.4 56.6 %all-gather.17.cloned.1.call-done = bf16[1024,1024]{1,0:T(8,128)(2,1)} async-done(((bf16[32,1024]{1,0:T(8,128)(2,1)}), bf16[1024,1024]{1,0:T(8,128)(2,1)}) %all-gather.17.cloned.1.call-update) | async-done | bytes 2097168 | tf_op jit(solution)/shard_map/all_gather | solution.py:174
  138.7 50.3 %all-gather.13.cloned.1.call-done = bf16[1024,1024]{1,0:T(8,128)(2,1)} async-done(((bf16[32,1024]{1,0:T(8,128)(2,1)}), bf16[1024,1024]{1,0:T(8,128)(2,1)}) %all-gather.13.cloned.1.call-update) | async-done | bytes 2097168 | tf_op jit(solution)/shard_map/all_gather | solution.py:175
  195.8 51.9 %all-gather.19.cloned.1.call-done = bf16[1024,1024]{1,0:T(8,128)(2,1)} async-done(((bf16[32,1024]{1,0:T(8,128)(2,1)}), bf16[1024,1024]{1,0:T(8,128)(2,1)}) %all-gather.19.cloned.1.call-update) | async-done | bytes 2097168 | tf_op jit(solution)/shard_map/all_gather | solution.py:176
  250.1 77.2 %all-gather.21.cloned.1.call-done = bf16[1024,4096]{1,0:T(8,128)(2,1)} async-done(((bf16[32,4096]{1,0:T(8,128)(2,1)}), bf16[1024,4096]{1,0:T(8,128)(2,1)}) %all-gather.21.cloned.1.call-update) | async-done | bytes 8388624 | tf_op jit(solution)/shard_map/all_gather | solution.py:178
  333.3 73.4 %all-gather.23.cloned.1.call-done = bf16[4096,1024]{1,0:T(8,128)(2,1)} async-done(((bf16[128,1024]{1,0:T(8,128)(2,1)}), bf16[4096,1024]{1,0:T(8,128)(2,1)}) %all-gather.23.cloned.1.call-update) | async-done | bytes 8388624 | tf_op jit(solution)/shard_map/all_gather | solution.py:179
  413.7 51.7 %all-gather.29.cloned.1.call-done = bf16[1024,1024]{1,0:T(8,128)(2,1)} async-done(((bf16[32,1024]{1,0:T(8,128)(2,1)}), bf16[1024,1024]{1,0:T(8,128)(2,1)}) %all-gather.29.cloned.1.call-update) | async-done | bytes 2097168 | tf_op jit(solution)/shard_map/all_gather | solution.py:203
  470.0 54.3 %all-gather.27.cloned.1.call-done = bf16[1024,1024]{1,0:T(8,128)(2,1)} async-done(((bf16[32,1024]{1,0:T(8,128)(2,1)}), bf16[1024,1024]{1,0:T(8,128)(2,1)}) %all-gather.27.cloned.1.call-update) | async-done | bytes 2097168 | tf_op jit(solution)/shard_map/all_gather | solution.py:202
  528.7 54.5 %all-gather.25.cloned.1.call-done = bf16[1024,1024]{1,0:T(8,128)(2,1)} async-done(((bf16[32,1024]{1,0:T(8,128)(2,1)}), bf16[1024,1024]{1,0:T(8,128)(2,1)}) %all-gather.25.cloned.1.call-update) | async-done | bytes 2097168 | tf_op jit(solution)/shard_map/all_gather | solution.py:204
  587.1 54.9 %all-gather.31.cloned.1.call-done = bf16[1024,1024]{1,0:T(8,128)(2,1)} async-done(((bf16[32,1024]{1,0:T(8,128)(2,1)}), bf16[1024,1024]{1,0:T(8,128)(2,1)}) %all-gather.31.cloned.1.call-update) | async-done | bytes 2097168 | tf_op jit(solution)/shard_map/all_gather | solution.py:205
  644.5 76.7 %all-gather.33.cloned.1.call-done = bf16[1024,4096]{1,0:T(8,128)(2,1)} async-done(((bf16[32,4096]{1,0:T(8,128)(2,1)}), bf16[1024,4096]{1,0:T(8,128)(2,1)}) %all-gather.33.cloned.1.call-update) | async-done | bytes 8388624 | tf_op jit(solution)/shard_map/all_gather | solution.py:207
  727.3 73.4 %all-gather.35.cloned.1.call-done = bf16[4096,1024]{1,0:T(8,128)(2,1)} async-done(((bf16[128,1024]{1,0:T(8,128)(2,1)}), bf16[4096,1024]{1,0:T(8,128)(2,1)}) %all-gather.35.cloned.1.call-update) | async-done | bytes 8388624 | tf_op jit(solution)/shard_map/all_gather | solution.py:208
  1063.5 40.3 %all-reduce.10 = (f32[1024]{0:T(1024)S(1)}, f32[1024]{0:T(1024)S(1)}, f32[1024]{0:T(1024)S(1)}, f32[1024]{0:T(1024)S(1)}, f32[1024]{0:T(1024)S(1)}) all-reduce(f32[1024]{0:T(1024)S(1)} %get-tuple-element.88, f32[1024]{0:T(1024)S(1)} %get-tuple-element.80, ...), channel_id=2, replica_groups=mesh['dp'=4,'fsdp'=8] {'dp','fsdp'}, use_global_device_ids=true, to_apply=%region_27.28.clone | all-reduce | flops 5120 | bytes 40960
  1124.8 22.7 reduce-scatter.15.cloned.1.call-done
  1149.1 140.4 %reduce-scatter.19.cloned.1.call-done = f32[256,128]{1,0:T(8,128)} async-done(((f32[8192,128]{1,0:T(8,128)}), f32[256,128]{1,0:T(8,128)}) %reduce-scatter.19.cloned.1.call-update) | async-done | bytes 131088 | tf_op jit(solution)/shard_map/reduce_scatter | solution.py:266
  1291.1 139.8 %reduce-scatter.31.cloned.1.call-done = f32[256,128]{1,0:T(8,128)} async-done(((f32[8192,128]{1,0:T(8,128)}), f32[256,128]{1,0:T(8,128)}) %reduce-scatter.31.cloned.1.call-update) | async-done | bytes 131088 | tf_op jit(solution)/shard_map/reduce_scatter | solution.py:274
  1432.4 140.0 %reduce-scatter.13.cloned.1.call-done = f32[256,128]{1,0:T(8,128)} async-done(((f32[8192,128]{1,0:T(8,128)}), f32[256,128]{1,0:T(8,128)}) %reduce-scatter.13.cloned.1.call-update) | async-done | bytes 131088 | tf_op jit(solution)/shard_map/reduce_scatter | solution.py:263
  1574.1 140.3 %reduce-scatter.29.cloned.1.call-done = f32[256,128]{1,0:T(8,128)} async-done(((f32[8192,128]{1,0:T(8,128)}), f32[256,128]{1,0:T(8,128)}) %reduce-scatter.29.cloned.1.call-update) | async-done | bytes 131088 | tf_op jit(solution)/shard_map/reduce_scatter | solution.py:273
  1716.0 140.5 %reduce-scatter.27.cloned.1.call-done = f32[256,128]{1,0:T(8,128)} async-done(((f32[8192,128]{1,0:T(8,128)}), f32[256,128]{1,0:T(8,128)}) %reduce-scatter.27.cloned.1.call-update) | async-done | bytes 131088 | tf_op jit(solution)/shard_map/reduce_scatter | solution.py:272
  1858.0 139.9 %reduce-scatter.25.cloned.1.call-done = f32[256,128]{1,0:T(8,128)} async-done(((f32[8192,128]{1,0:T(8,128)}), f32[256,128]{1,0:T(8,128)}) %reduce-scatter.25.cloned.1.call-update) | async-done | bytes 131088 | tf_op jit(solution)/shard_map/reduce_scatter | solution.py:271
  1999.5 184.1 %reduce-scatter.23.cloned.1.call-done = f32[1024,128]{1,0:T(8,128)} async-done(((f32[32768,128]{1,0:T(8,128)}), f32[1024,128]{1,0:T(8,128)}) %reduce-scatter.23.cloned.1.call-update) | async-done | bytes 524304 | tf_op jit(solution)/shard_map/reduce_scatter | solution.py:269
  2185.6 184.8 %reduce-scatter.35.cloned.1.call-done = f32[1024,128]{1,0:T(8,128)} async-done(((f32[32768,128]{1,0:T(8,128)}), f32[1024,128]{1,0:T(8,128)}) %reduce-scatter.35.cloned.1.call-update) | async-done | bytes 524304 | tf_op jit(solution)/shard_map/reduce_scatter | solution.py:277
  2372.3 184.8 %reduce-scatter.21.cloned.1.call-done = f32[256,512]{1,0:T(8,128)} async-done(((f32[8192,512]{1,0:T(8,128)}), f32[256,512]{1,0:T(8,128)}) %reduce-scatter.21.cloned.1.call-update) | async-done | bytes 524304 | tf_op jit(solution)/shard_map/reduce_scatter | solution.py:268
  2559.0 184.6 %reduce-scatter.33.cloned.1.call-done = f32[256,512]{1,0:T(8,128)} async-done(((f32[8192,512]{1,0:T(8,128)}), f32[256,512]{1,0:T(8,128)}) %reduce-scatter.33.cloned.1.call-update) | async-done | bytes 524304 | tf_op jit(solution)/shard_map/reduce_scatter | solution.py:276
  (343 shorter events, 376.6 us)
Async XLA Ops:
  7.3 63.8 %all-gather.15.cloned.1.call-start = ((), (), s32[]{:S(2)}) async-start(), calls=%async_computation.13 | async-start | bytes 2162688 | tf_op jit(solution)/shard_map/all_gather | solution.py:173
  9.0 121.1 %all-gather.17.cloned.1.call-start = ((), (), s32[]{:S(2)}) async-start(), calls=%async_computation.14 | async-start | bytes 2162688 | tf_op jit(solution)/shard_map/all_gather | solution.py:174
  10.6 178.4 %all-gather.13.cloned.1.call-start = ((), (), s32[]{:S(2)}) async-start(), calls=%async_computation.12 | async-start | bytes 2162688 | tf_op jit(solution)/shard_map/all_gather | solution.py:175
  12.2 235.5 %all-gather.19.cloned.1.call-start = ((), (), s32[]{:S(2)}) async-start(), calls=%async_computation.15 | async-start | bytes 2162688 | tf_op jit(solution)/shard_map/all_gather | solution.py:176
  13.8 313.5 %all-gather.21.cloned.1.call-start = ((), (), s32[]{:S(2)}) async-start(), calls=%async_computation.16 | async-start | bytes 8650752 | tf_op jit(solution)/shard_map/all_gather | solution.py:178
  15.8 390.9 %all-gather.23.cloned.1.call-start = ((), (), s32[]{:S(2)}) async-start(), calls=%async_computation.17 | async-start | bytes 8650752 | tf_op jit(solution)/shard_map/all_gather | solution.py:179
  16.6 448.8 %all-gather.29.cloned.1.call-start = ((), (), s32[]{:S(2)}) async-start(), calls=%async_computation.20 | async-start | bytes 2162688 | tf_op jit(solution)/shard_map/all_gather | solution.py:203
  17.4 506.9 %all-gather.27.cloned.1.call-start = ((), (), s32[]{:S(2)}) async-start(), calls=%async_computation.19 | async-start | bytes 2162688 | tf_op jit(solution)/shard_map/all_gather | solution.py:202
  18.1 565.1 %all-gather.25.cloned.1.call-start = ((), (), s32[]{:S(2)}) async-start(), calls=%async_computation.18 | async-start | bytes 2162688 | tf_op jit(solution)/shard_map/all_gather | solution.py:204
  18.9 623.2 %all-gather.31.cloned.1.call-start = ((), (), s32[]{:S(2)}) async-start(), calls=%async_computation.21 | async-start | bytes 2162688 | tf_op jit(solution)/shard_map/all_gather | solution.py:205
  19.6 701.7 %all-gather.33.cloned.1.call-start = ((), (), s32[]{:S(2)}) async-start(), calls=%async_computation.22 | async-start | bytes 8650752 | tf_op jit(solution)/shard_map/all_gather | solution.py:207
  20.4 780.3 %all-gather.35.cloned.1.call-start = ((), (), s32[]{:S(2)}) async-start(), calls=%async_computation.23 | async-start | bytes 8650752 | tf_op jit(solution)/shard_map/all_gather | solution.py:208
  21.2 1102.0 %reduce-scatter.17.cloned.1.call-start = ((), (), s32[]{:S(2)}) async-start(), calls=%async_computation.26 | async-start | bytes 4325376 | tf_op jit(solution)/shard_map/reduce_scatter | solution.py:265
  864.5 283.0 %reduce-scatter.15.cloned.1.call-start = ((), (), s32[]{:S(2)}) async-start(), calls=%async_computation.25 | async-start | bytes 4325376 | tf_op jit(solution)/shard_map/reduce_scatter | solution.py:264
  881.9 407.6 %reduce-scatter.19.cloned.1.call-start = ((), (), s32[]{:S(2)}) async-start(), calls=%async_computation.27 | async-start | bytes 4325376 | tf_op jit(solution)/shard_map/reduce_scatter | solution.py:266
  890.6 540.2 %reduce-scatter.31.cloned.1.call-start = ((), (), s32[]{:S(2)}) async-start(), calls=%async_computation.33 | async-start | bytes 4325376 | tf_op jit(solution)/shard_map/reduce_scatter | solution.py:274
  899.4 673.1 %reduce-scatter.13.cloned.1.call-start = ((), (), s32[]{:S(2)}) async-start(), calls=%async_computation.24 | async-start | bytes 4325376 | tf_op jit(solution)/shard_map/reduce_scatter | solution.py:263
  913.5 800.9 %reduce-scatter.29.cloned.1.call-start = ((), (), s32[]{:S(2)}) async-start(), calls=%async_computation.32 | async-start | bytes 4325376 | tf_op jit(solution)/shard_map/reduce_scatter | solution.py:273
  922.2 934.3 %reduce-scatter.27.cloned.1.call-start = ((), (), s32[]{:S(2)}) async-start(), calls=%async_computation.31 | async-start | bytes 4325376 | tf_op jit(solution)/shard_map/reduce_scatter | solution.py:272
  930.9 1067.1 %reduce-scatter.25.cloned.1.call-start = ((), (), s32[]{:S(2)}) async-start(), calls=%async_computation.30 | async-start | bytes 4325376 | tf_op jit(solution)/shard_map/reduce_scatter | solution.py:271
  939.6 1244.0 %reduce-scatter.23.cloned.1.call-start = ((), (), s32[]{:S(2)}) async-start(), calls=%async_computation.29 | async-start | bytes 17301504 | tf_op jit(solution)/shard_map/reduce_scatter | solution.py:269
  967.7 1402.6 %reduce-scatter.35.cloned.1.call-start = ((), (), s32[]{:S(2)}) async-start(), calls=%async_computation.35 | async-start | bytes 17301504 | tf_op jit(solution)/shard_map/reduce_scatter | solution.py:277
  995.6 1561.5 %reduce-scatter.21.cloned.1.call-start = ((), (), s32[]{:S(2)}) async-start(), calls=%async_computation.28 | async-start | bytes 17301504 | tf_op jit(solution)/shard_map/reduce_scatter | solution.py:268
  1023.3 1720.3 %reduce-scatter.33.cloned.1.call-start = ((), (), s32[]{:S(2)}) async-start(), calls=%async_computation.34 | async-start | bytes 17301504 | tf_op jit(solution)/shard_map/reduce_scatter | solution.py:276
  (64 other events, 621.9 us)
Sparse Core Ops, SparseCore 0:
  11.6 59.4 all-gather.14
  74.7 55.3 all-gather.16
  133.6 55.3 all-gather.12
  192.4 55.3 all-gather.18
  251.1 76.1 all-gather.20
  330.7 75.9 all-gather.22
  410.3 55.0 all-gather.28
  468.9 55.3 all-gather.26
  527.9 55.3 all-gather.24
  586.6 55.3 all-gather.30
  645.0 76.2 all-gather.32
  724.7 75.9 all-gather.34
  864.6 141.3 reduce-scatter.16
  1008.1 139.3 reduce-scatter.14
  1149.6 139.8 reduce-scatter.18
  1291.6 139.1 reduce-scatter.30
  1433.0 139.4 reduce-scatter.12
  1574.6 139.7 reduce-scatter.28
  1716.7 139.7 reduce-scatter.26
  1858.6 139.3 reduce-scatter.24
  2000.2 183.3 reduce-scatter.22
  2186.0 184.3 reduce-scatter.34
  2372.7 184.3 reduce-scatter.20
  2559.2 184.3 reduce-scatter.32
where the time goes:
time: 2760 us; the launch traced here: 2750 us
  waiting for transfers between devices  2280 us (83%)
  matrix products  177 us (6%)
  local copies, waits for them, and re-layouts  168 us (6%)
  blocking collectives  82.7 us (3%)
  other arithmetic  28.5 us (1%)
    reduce_scatter x1, waiting for transfers between devices, local(): lax.psum_scatter(widen(grad_down_two), ('dp', 'fsdp'), scatter_dimension=...  185 us
    reduce_scatter x1, waiting for transfers between devices, local(): lax.psum_scatter(widen(grad_up_one), ('dp', 'fsdp'), scatter_dimension=0,...  185 us
    reduce_scatter x1, waiting for transfers between devices, local(): lax.psum_scatter(widen(grad_up_two), ('dp', 'fsdp'), scatter_dimension=0,...  185 us
    reduce_scatter x1, waiting for transfers between devices, local(): lax.psum_scatter(widen(grad_down_one), ('dp', 'fsdp'), scatter_dimension=...  184 us
    reduce_scatter x1, waiting for transfers between devices, local(): lax.psum_scatter(widen(grad_s_key), ('dp', 'fsdp'), scatter_dimension=0,...  140 us
    reduce_scatter x1, waiting for transfers between devices, local(): lax.psum_scatter(widen(grad_w_out), ('dp', 'fsdp'), scatter_dimension=0,...  140 us
    reduce_scatter x1, waiting for transfers between devices, local(): lax.psum_scatter(widen(grad_s_value), ('dp', 'fsdp'), scatter_dimension=0...  140 us
    reduce_scatter x1, waiting for transfers between devices, local(): lax.psum_scatter(widen(grad_w_query), ('dp', 'fsdp'), scatter_dimension=0...  140 us
  transfers between devices with their start and end apart: 24, of which 23 were waited for; matrix products, arithmetic and copies ran while one was open for 11% of the time, Pallas kernels for 0%

commit v1 on v0

--- a/solution.py
+++ b/solution.py
@@ -1,3 +1,5 @@
+import functools
+
 import jax
 import jax.numpy as jnp
 from jax import lax
@@ -9,7 +11,6 @@
 
 EPS = 1e-05
 NEG = -1000000000.0
-FOLD = 8
 
 
 def layer_norm(value, gain):
@@ -36,14 +37,6 @@
     return lax.dot_general(
         grad, weight, (((1,), (1,)), ((), ())), preferred_element_type=jnp.float32
     )
-
-
-def widen(value):
-    return value.reshape(value.shape[0] * FOLD, value.shape[1] // FOLD)
-
-
-def narrow(value, columns):
-    return value.reshape(-1, columns)
 
 
 def norm_back(value, gain, grad):
@@ -162,23 +155,36 @@
     second_up,
     second_down,
     cotangent,
+    mesh_size,
 ):
     groups, lat_rows, width = latents.shape
     span = inputs.shape[1]
     hidden_width = first_up.shape[1]
     low_type = jnp.bfloat16
-    cross_set = (
-        lax.all_gather(norm_latent.astype(low_type), ("dp", "fsdp"), axis=0, tiled=True),
-        lax.all_gather(norm_input.astype(low_type), ("dp", "fsdp"), axis=0, tiled=True),
-        lax.all_gather(cross_query.astype(low_type), ("dp", "fsdp"), axis=0, tiled=True),
-        lax.all_gather(cross_key.astype(low_type), ("dp", "fsdp"), axis=0, tiled=True),
-        lax.all_gather(cross_value.astype(low_type), ("dp", "fsdp"), axis=0, tiled=True),
-        lax.all_gather(cross_output.astype(low_type), ("dp", "fsdp"), axis=0, tiled=True),
-        lax.all_gather(norm_first.astype(low_type), ("dp", "fsdp"), axis=0, tiled=True),
-        lax.all_gather(first_up.astype(low_type), ("dp", "fsdp"), axis=0, tiled=True),
-        lax.all_gather(first_down.astype(low_type), ("dp", "fsdp"), axis=0, tiled=True),
-    )
-    gain_lat, gain_inp, w_query, w_key, w_value, w_out, gain_first, up_one, down_one = cross_set
+    parts = mesh_size
+    gains = (norm_latent, norm_input, norm_first, norm_self, norm_second)
+    mats = (cross_query, cross_key, cross_value, cross_output, first_up, first_down,
+            self_query, self_key, self_value, self_output, second_up, second_down)
+    blocks = []
+    for mat in mats:
+        for start in range(0, mat.shape[1], width):
+            blocks.append(mat[:, start:start + width])
+    gain_row = jnp.concatenate([jnp.concatenate(gains), jnp.zeros((width - 5 * gains[0].shape[0],), jnp.float32)])
+    gain_rows = jnp.concatenate([gain_row[None], jnp.zeros((15, width), jnp.float32)])
+    packed = jnp.concatenate([gain_rows] + blocks).astype(low_type)
+    whole = lax.all_gather(packed, ("dp", "fsdp"), axis=0, tiled=False)
+    per = gains[0].shape[0]
+    gathered_gains = [whole[:, 0, i * per:(i + 1) * per].reshape(width) for i in range(5)]
+    gain_lat, gain_inp, gain_first, gain_self, gain_second = gathered_gains
+    at = 16
+    full = []
+    for mat in mats:
+        columns = []
+        for start in range(0, mat.shape[1], width):
+            columns.append(whole[:, at:at + mat.shape[0]].reshape(parts * mat.shape[0], width))
+            at += mat.shape[0]
+        full.append(columns[0] if len(columns) == 1 else jnp.concatenate(columns, axis=1))
+    w_query, w_key, w_value, w_out, up_one, down_one, s_query, s_key, s_value, s_out, up_two, down_two = full
     positions = jnp.arange(span, dtype=jnp.int32)
     valid = positions[None, :] < (frames * FRAME_TOK)[:, None]
     every = jnp.ones((groups, lat_rows), dtype=bool)
@@ -197,17 +203,6 @@
     )
     first_resid = latent_rows + product(mixed_one, w_out)
     second_resid, saved_one = feed_forward(first_resid, gain_first, up_one, down_one)
-    self_set = (
-        lax.all_gather(norm_self.astype(low_type), ("dp", "fsdp"), axis=0, tiled=True),
-        lax.all_gather(self_query.astype(low_type), ("dp", "fsdp"), axis=0, tiled=True),
-        lax.all_gather(self_key.astype(low_type), ("dp", "fsdp"), axis=0, tiled=True),
-        lax.all_gather(self_value.astype(low_type), ("dp", "fsdp"), axis=0, tiled=True),
-        lax.all_gather(self_output.astype(low_type), ("dp", "fsdp"), axis=0, tiled=True),
-        lax.all_gather(norm_second.astype(low_type), ("dp", "fsdp"), axis=0, tiled=True),
-        lax.all_gather(second_up.astype(low_type), ("dp", "fsdp"), axis=0, tiled=True),
-        lax.all_gather(second_down.astype(low_type), ("dp", "fsdp"), axis=0, tiled=True),
-    )
-    gain_self, s_query, s_key, s_value, s_out, gain_second, up_two, down_two = self_set
     normed_self = layer_norm(second_resid, gain_self.astype(jnp.float32)).astype(low_type)
     query_two = product(normed_self, s_query).astype(low_type)
     key_two = product(normed_self, s_key).astype(low_type)
@@ -257,48 +252,34 @@
     grad_input_rows, grad_gain_inp = norm_back(
         input_rows, gain_inp.astype(jnp.float32), grad_normed_inp
     )
-    every_sum = (
-        lax.psum_scatter(grad_gain_lat, ("dp", "fsdp"), scatter_dimension=0, tiled=True),
-        lax.psum_scatter(grad_gain_inp, ("dp", "fsdp"), scatter_dimension=0, tiled=True),
-        lax.psum_scatter(widen(grad_w_query), ("dp", "fsdp"), scatter_dimension=0, tiled=True),
-        lax.psum_scatter(widen(grad_w_key), ("dp", "fsdp"), scatter_dimension=0, tiled=True),
-        lax.psum_scatter(widen(grad_w_value), ("dp", "fsdp"), scatter_dimension=0, tiled=True),
-        lax.psum_scatter(widen(grad_w_out), ("dp", "fsdp"), scatter_dimension=0, tiled=True),
-        lax.psum_scatter(grad_gain_first, ("dp", "fsdp"), scatter_dimension=0, tiled=True),
-        lax.psum_scatter(widen(grad_up_one), ("dp", "fsdp"), scatter_dimension=0, tiled=True),
-        lax.psum_scatter(widen(grad_down_one), ("dp", "fsdp"), scatter_dimension=0, tiled=True),
-        lax.psum_scatter(grad_gain_self, ("dp", "fsdp"), scatter_dimension=0, tiled=True),
-        lax.psum_scatter(widen(grad_s_query), ("dp", "fsdp"), scatter_dimension=0, tiled=True),
-        lax.psum_scatter(widen(grad_s_key), ("dp", "fsdp"), scatter_dimension=0, tiled=True),
-        lax.psum_scatter(widen(grad_s_value), ("dp", "fsdp"), scatter_dimension=0, tiled=True),
-        lax.psum_scatter(widen(grad_s_out), ("dp", "fsdp"), scatter_dimension=0, tiled=True),
-        lax.psum_scatter(grad_gain_second, ("dp", "fsdp"), scatter_dimension=0, tiled=True),
-        lax.psum_scatter(widen(grad_up_two), ("dp", "fsdp"), scatter_dimension=0, tiled=True),
-        lax.psum_scatter(widen(grad_down_two), ("dp", "fsdp"), scatter_dimension=0, tiled=True),
-    )
+    grad_mats = (grad_w_query, grad_w_key, grad_w_value, grad_w_out, grad_up_one, grad_down_one,
+                 grad_s_query, grad_s_key, grad_s_value, grad_s_out, grad_up_two, grad_down_two)
+    gain_grads = jnp.stack([grad_gain_lat, grad_gain_inp, grad_gain_first, grad_gain_self, grad_gain_second])
+    gain_grads = jnp.moveaxis(gain_grads.reshape(5, parts, per), 1, 0).reshape(parts, 1, 5 * per)
+    gain_grads = jnp.pad(gain_grads, ((0, 0), (0, 15), (0, width - 5 * per)))
+    pieces = [gain_grads.astype(low_type)]
+    for grad in grad_mats:
+        for start in range(0, grad.shape[1], width):
+            pieces.append(grad[:, start:start + width].reshape(parts, -1, width).astype(low_type))
+    summed = lax.psum_scatter(jnp.concatenate(pieces, axis=1), ("dp", "fsdp"), scatter_dimension=0, tiled=False)
+    summed = summed.astype(jnp.float32)
+    gain_out = [summed[0, i * per:(i + 1) * per] for i in range(5)]
+    at = 16
+    out = []
+    for mat in mats:
+        columns = []
+        for start in range(0, mat.shape[1], width):
+            columns.append(summed[at:at + mat.shape[0]])
+            at += mat.shape[0]
+        out.append(columns[0] if len(columns) == 1 else jnp.concatenate(columns, axis=1))
     grad_latents = grad_latent_rows.reshape(groups, lat_rows, width).astype(low_type)
     grad_inputs = grad_input_rows.reshape(groups, span, width).astype(low_type)
     return (
-        result,
-        grad_latents,
-        grad_inputs,
-        every_sum[0],
-        every_sum[1],
-        narrow(every_sum[2], width),
-        narrow(every_sum[3], width),
-        narrow(every_sum[4], width),
-        narrow(every_sum[5], width),
-        every_sum[6],
-        narrow(every_sum[7], hidden_width),
-        narrow(every_sum[8], width),
-        every_sum[9],
-        narrow(every_sum[10], width),
-        narrow(every_sum[11], width),
-        narrow(every_sum[12], width),
-        narrow(every_sum[13], width),
-        every_sum[14],
-        narrow(every_sum[15], hidden_width),
-        narrow(every_sum[16], width),
+        result, grad_latents, grad_inputs,
+        gain_out[0], gain_out[1], out[0], out[1], out[2], out[3],
+        gain_out[2], out[4], out[5],
+        gain_out[3], out[6], out[7], out[8], out[9],
+        gain_out[4], out[10], out[11],
     )
 
 
@@ -348,4 +329,4 @@
         P(("dp", "fsdp"), None),
         P(("dp", "fsdp"), None),
     )
-    return jax.shard_map(local, mesh=mesh, in_specs=in_specs, out_specs=out_specs, check_vma=False)
+    return jax.shard_map(functools.partial(local, mesh_size=mesh.size), mesh=mesh, in_specs=in_specs, out_specs=out_specs, check_vma=False)

time: 2760 us -> 1120 us (0.41)
  waiting for transfers between devices: 2280 us -> 812 us
  blocking collectives: 82.7 us -> 0 us
  local copies, waits for them, and re-layouts: 168 us -> 120 us
  matrix products: 177 us -> 137 us
    reduce_scatter x12 -> x1, waiting for transfers between devices: 1600 us -> 534 us  [local(): lax.psum_scatter(jnp.concatenate(pieces, axis=1), ('dp', 'fsdp'), scatter...]
    all_gather x12 -> x1, waiting for transfers between devices: 676 us -> 278 us  [local(): whole = lax.all_gather(packed, ('dp', 'fsdp'), axis=0, tiled=False)]
    reshape x24 -> x1, local copies, waits for them, and re-layouts: 132 us -> 0.1 us  [local(): jnp.moveaxis(gain_grads.reshape(5, parts, per), 1, 0)]
    unnamed x2 -> x0, blocking collectives: 82.7 us -> none
    slice x0 -> x6, local copies, waits for them, and re-layouts: none -> 46.9 us  [the longest x2 33.1 us: local(): whole[:, at:at + mat.shape[0]].reshape(parts * mat.shape[0], width)]
  transfers between devices with their start and end apart: 24 -> 2, of which waited for: 23 -> 2; matrix products, arithmetic and copies ran while one was open for 11% -> 1% of each run, Pallas kernels for 0% -> 0%
where the time goes in v1:
time: 1120 us; the launch traced here: 1110 us
  waiting for transfers between devices  812 us (72%)
  matrix products  137 us (12%)
  local copies, waits for them, and re-layouts  120 us (11%)
  other arithmetic  26.3 us (2%)
  between operations  16 us (1%)
    reduce_scatter x1, waiting for transfers between devices, local(): lax.psum_scatter(jnp.concatenate(pieces, axis=1), ('dp', 'fsdp'), scatter...  534 us
    all_gather x1, waiting for transfers between devices, local(): whole = lax.all_gather(packed, ('dp', 'fsdp'), axis=0, tiled=False)  278 us
    dot_general x12, matrix products, weight_grad(): lax.dot_general(left, right, (((0,), (0,)), ((), ())), preferred_element_...  45.9 us
    unnamed x196, local copies, waits for them, and re-layouts  45.8 us
    dot_general x12, matrix products, product(): return jnp.dot(left, right, preferred_element_type=jnp.float32)  37.2 us
    dot_general x12, matrix products, back_product(): lax.dot_general(grad, weight, (((1,), (1,)), ((), ())), preferred_element...  34.6 us
    slice x2, local copies, waits for them, and re-layouts, local(): whole[:, at:at + mat.shape[0]].reshape(parts * mat.shape[0], width)  33.1 us
  transfers between devices with their start and end apart: 2, of which 2 were waited for; matrix products, arithmetic and copies ran while one was open for 1% of the time, Pallas kernels for 0%

profile of v1, /device:TPU:0, one launch (start us, length us, event | category | flops | bytes accessed | tf_op | source)
XLA Modules:
  0.0 1111.7 jit_solution(15814612884760590458)
XLA Ops:
  15.2 13.7 %concatenate.90 = bf16[1,784,1024]{2,1,0:T(8,128)(2,1)} concatenate(bf16[1,1,1024]{2,1,0:T(2,128)(2,1)S(1)} %concatenate.71, bf16[1,15,1024]{2,1,0:T(8,128)(2,1)S(1)} %broadcast_in_dim.53, bf16[1,32,1024]{2,1,0:T(8,128)(2,1)S(1)} %get-tuple-element.200, bf16[1,32,1024]{2,1,0:T(8,128)(2,1)S(1)} %get-tuple-element.199, bf16[1,32,1024]{2,1,0:T(8,128)(2,1)S(1)} %get-tuple-element.198, ...), dimensions={1} | concatenate | bytes 3211264 | tf_op jit(solution)/shard_map/concatenate | solution.py:174
  34.5 278.0 %all-gather.2.cloned.1.call-done = bf16[32,784,1024]{2,1,0:T(8,128)(2,1)} async-done(((bf16[1,784,1024]{2,1,0:T(8,128)(2,1)}), bf16[32,784,1024]{2,1,0:T(8,128)(2,1)}) %all-gather.2.cloned.1.call-update) | async-done | bytes 51380240 | tf_op jit(solution)/shard_map/all_gather | solution.py:175
  314.1 22.3 %fusion.134 = (bf16[32,32,1024]{2,1,0:T(8,128)(2,1)}, bf16[32,32,1024]{2,1,0:T(8,128)(2,1)}, bf16[32,32,1024]{2,1,0:T(8,128)(2,1)}, bf16[32,32,1024]{2,1,0:T(8,1...) fusion(bf16[32,784,1024]{2,1,0:T(8,128)(2,1)} %all-gather.2.clo, ...), kind=kLoop, calls=%fused_computation.295 | loop fusion | bytes 67108864 | tf_op jit(solution)/shard_map/slice | solution.py:184
  338.4 5.7 convolution_convert_fusion.4
  344.1 4.0 convolution_convert_fusion.3
  356.4 4.3 fusion.50
  360.7 10.8 fusion.135
  386.1 6.5 fusion.37
  394.0 3.7 fusion.29
  411.7 3.3 fusion.144
  421.5 7.3 fusion.22
  437.0 4.3 multiply_reduce_fusion
  448.5 5.8 convolution_convert_fusion.2
  454.4 5.6 convolution_convert_fusion.1
  461.1 5.8 convolution_convert_fusion
  485.1 6.2 fusion.137
  491.4 5.7 fusion.136
  499.9 3.3 convert_dynamic-update-slice_fusion.8
  503.2 5.5 convert_dynamic-update-slice_fusion.7
  508.7 3.7 convert_dynamic-update-slice_fusion.6
  523.1 8.3 constant_dynamic-update-slice_fusion.9
  547.6 5.9 convert_dynamic-update-slice_fusion
  557.6 6.8 fusion.60
  564.4 533.8 %reduce-scatter.2.cloned.1.call-done = bf16[1,784,1024]{2,1,0:T(8,128)(2,1)} async-done(((bf16[32,784,1024]{2,1,0:T(8,128)(2,1)}), bf16[1,784,1024]{2,1,0:T(8,128)(2,1)}) %reduce-scatter.2.cloned.1.call-update) | async-done | bytes 1605648 | tf_op jit(solution)/shard_map/reduce_scatter | solution.py:264
  (325 shorter events, 135.4 us)
Async XLA Ops:
  7.2 7.8 copy-start.79
  7.2 7.8 copy-start.80
  7.2 305.3 %all-gather.2.cloned.1.call-start = ((), (), s32[]{:S(2)}) async-start(), calls=%async_computation.1 | async-start | bytes 52985856 | tf_op jit(solution)/shard_map/all_gather | solution.py:175
  28.9 1069.3 %reduce-scatter.2.cloned.1.call-start = ((), (), s32[]{:S(2)}) async-start(), calls=%async_computation.2 | async-start | bytes 52985856 | tf_op jit(solution)/shard_map/reduce_scatter | solution.py:264
  338.4 9.8 copy-start.33
  356.1 15.4 %copy-start.11 = (f32[128,1024]{1,0:T(8,128)}, f32[128,1024]{1,0:T(8,128)S(1)}, u32[]{:S(2)}) copy-start(f32[128,1024]{1,0:T(8,128)S(1)} %get-tuple-element.167) | copy-start | bytes 1572868
  360.7 10.8 copy-start.25
  383.5 10.5 slice-start
  385.9 14.9 %copy-start.9 = (f32[128,1024]{1,0:T(8,128)}, f32[128,1024]{1,0:T(8,128)S(1)}, u32[]{:S(2)}) copy-start(f32[128,1024]{1,0:T(8,128)S(1)} %get-tuple-element.173) | copy-start | bytes 1572868
  386.1 7.9 slice-start.1
  386.1 7.9 copy-start.36
  411.7 7.1 copy-start.47
  421.5 10.7 copy-start.28
  421.5 7.4 copy-start.12
  421.5 7.4 copy-start.55
  421.5 7.4 copy-start.56
  421.5 7.4 copy-start.57
  421.5 7.4 copy-start.58
  448.5 5.8 copy-start.27
  448.5 5.8 copy-start.29
  454.4 6.7 copy-start.10
  454.4 6.7 copy-start.69
  485.1 6.2 copy-start.74
  523.1 8.3 copy-start.48
  (68 other events, 177.9 us)
Sparse Core Ops, SparseCore 0:
  29.1 283.4 all-gather.1
  553.6 544.5 reduce-scatter.1
